TPU v7x, 256 devices: a whole 4x4x8 slice. The times are simulated.
256 devices in a mesh: group: 32 (over y_hi, z, core), shard: 4 (over x), tensor: 2 (over y_lo).
Axes of the slice: x: 4, y: 4 (y_hi: 2, y_lo: 2; y = y_hi * 2 + y_lo), z: 8, core: 2. Of those that a mesh axis runs over, the one named last changes fastest.
Arguments:
- partials: bfloat16 [12288, 2, 16384], P('group', 'tensor', 'shard'), may hold values from -10 to 10
- index_map: int32 [128, 4], replicated, may hold values from 0 to 31
- sign_bits: int32 [16384], replicated, may hold values from 0 to 1
- blocks: bfloat16 [4, 128, 128], replicated, may hold values from -0.125 to 0.125
Outputs:
- sketch: bfloat16 [12288, 4096], P(('group', 'shard', 'tensor'))
- kernel: float32 [32, 384, 12288], P(None, ('shard', 'tensor'), 'group')
All inputs are finite; a program needn't handle non-finite values.
Results may differ from a plain program's by a relative error of at most 0.014.
Values may be sent and summed in bfloat16 or wider, within the bound.
A program may use at most 128 MiB of HBM per device.

v0:
```python
import jax
import jax.numpy as jnp
from jax import lax
from jax.sharding import PartitionSpec as P

SKETCH = 4096
BLOCK = 128


def shifted(value, axis, steps):
    count = lax.axis_size(axis)
    pairs = [(source, (source + steps) % count) for source in range(count)]
    return lax.ppermute(value, axis, pairs)


def split_pair(values):
    upper = values.astype(jnp.bfloat16)
    lower = (values - upper.astype(jnp.float32)).astype(jnp.bfloat16)
    return (upper, lower)


def project_float(signed, blocks):
    upper, lower = split_pair(signed)
    first = jnp.einsum("ebc,jcd->ebjd", upper, blocks, preferred_element_type=jnp.float32)
    return first + jnp.einsum("ebc,jcd->ebjd", lower, blocks, preferred_element_type=jnp.float32)


def fold_blocks(projected, part_map):
    sketch_blocks = SKETCH // BLOCK
    onehot = (
        part_map[:, :, None] == jnp.arange(sketch_blocks, dtype=jnp.int32)[None, None, :]
    ).astype(jnp.bfloat16)
    upper, lower = split_pair(projected)
    summed = jnp.einsum("ebjd,bjs->esd", upper, onehot, preferred_element_type=jnp.float32)
    summed = summed + jnp.einsum("ebjd,bjs->esd", lower, onehot, preferred_element_type=jnp.float32)
    return summed.reshape(-1, SKETCH)


def on_device(partials, index_map, sign_bits, blocks):
    shard_index = lax.axis_index("shard")
    shard_width = partials.shape[2]
    own_rows = partials[:, 0, :]
    tensor_count = lax.axis_size("tensor")
    tensor_index = lax.axis_index("tensor")
    half_width = shard_width // tensor_count
    block_count = half_width // BLOCK
    gradient = lax.psum_scatter(
        own_rows.astype(jnp.float32).astype(jnp.bfloat16), "tensor", scatter_dimension=1, tiled=True
    ).astype(jnp.float32)
    first_param = shard_index * shard_width + tensor_index * half_width
    part_map = lax.dynamic_slice_in_dim(index_map, first_param // BLOCK, block_count, 0)
    part_signs = lax.dynamic_slice_in_dim(sign_bits, first_param, half_width, 0)
    sign_rows = (2 * part_signs - 1).astype(jnp.float32).reshape(block_count, BLOCK)
    signed = gradient.reshape(-1, block_count, BLOCK) * sign_rows[None]
    partial_sketch = fold_blocks(project_float(signed, blocks), part_map)
    own_sum = lax.psum_scatter(partial_sketch, ("shard", "tensor"), scatter_dimension=0, tiled=True)
    own_sketch = own_sum.astype(jnp.bfloat16)
    row_sketch = lax.all_gather(own_sketch, ("shard", "tensor"), axis=0, tiled=True)
    groups = lax.axis_size("group")
    position = lax.axis_index("group")
    zero_index = jnp.zeros((), jnp.int32)

    def tile_block(moving):
        return (
            lax.dot_general(
                moving, row_sketch, (((1,), (1,)), ((), ())), preferred_element_type=jnp.float32
            )
            / SKETCH
        )

    def place(kernel, moving, source):
        return lax.dynamic_update_slice(
            kernel, tile_block(moving)[None], (source, zero_index, zero_index)
        )

    kernel = jnp.zeros((groups, own_sketch.shape[0], row_sketch.shape[0]), jnp.float32)
    kernel = place(kernel, own_sketch, position)

    def advance(turn_index, state_pair):
        moving, kernel_now = state_pair
        moving = shifted(moving, "group", 1)
        source = (position - turn_index) % groups
        return (moving, place(kernel_now, moving, source))

    final_pair = lax.fori_loop(1, groups, advance, (own_sketch, kernel))
    kernel = final_pair[1]
    return (own_sketch, kernel)


def solution(mesh):
    placed = (P("group", "tensor", "shard"), P(), P(), P())
    return jax.shard_map(
        on_device,
        mesh=mesh,
        in_specs=placed,
        out_specs=(P(("group", "shard", "tensor"), None), P(None, ("shard", "tensor"), "group")),
        check_vma=False,
    )
```

profile of v0, /device:TPU:1, one launch (start us, length us, event | category | flops | bytes accessed | tf_op | source)
XLA Modules:
  0.0 786.9 jit_solution(16908089562517089834)
XLA Ops:
  8.8 54.0 %reduce-scatter.3.cloned.1.call-done = bf16[384,2048]{1,0:T(8,128)(2,1)} async-done(((bf16[384,4096]{1,0:T(8,128)(2,1)}), bf16[384,2048]{1,0:T(8,128)(2,1)}) %reduce-scatter.3.cloned.1.call-update) | async-done | bytes 1572880 | tf_op jit(solution)/shard_map/reduce_scatter | solution.py:47
  62.8 3.3 fusion.13
  66.1 5.9 add_convert_fusion
  72.0 7.2 fusion.2
  79.2 4.5 bitcast_add_fusion
  83.7 8.8 %copy.37 = f32[48,8,32,128]{3,1,2,0:T(8,128)} copy(f32[48,8,32,128]{3,2,1,0:T(8,128)S(1)} %bitcast.78) | data formatting | bytes 12582912
  92.6 133.4 %reduce-scatter.5.cloned.1.call-done = f32[48,4096]{1,0:T(8,128)} async-done(((f32[384,4096]{1,0:T(8,128)}), f32[48,4096]{1,0:T(8,128)}) %reduce-scatter.5.cloned.1.call-update) | async-done | bytes 786448 | tf_op jit(solution)/shard_map/reduce_scatter | solution.py:56
  229.7 72.4 %all-gather.2.cloned.1.call-done = bf16[384,4096]{1,0:T(8,128)(2,1)} async-done(((bf16[48,4096]{1,0:T(8,128)(2,1)}), bf16[384,4096]{1,0:T(8,128)(2,1)}) %all-gather.2.cloned.1.call-update) | async-done | bytes 3145744 | tf_op jit(solution)/shard_map/all_gather | solution.py:58
  302.3 3.2 fusion.18
  306.9 473.5 %while.17 = (s32[]{:T(128)}, bf16[48,4096]{1,0:T(8,128)(2,1)}, f32[32,48,384]{2,1,0:T(8,128)}, bf16[384,4096]{1,0:T(8,128)(2,1)S(1)}, s32[]{:T(128)}, /*index=5*/s32[]{:T(128)}, s32[]{:T(128)}, s32[]{:T(128)}, s32[]{:T(128)}) while((s32[]{:T(128)}, bf16[48,4096]{1,0:T(8,128)(2,1)}, f32[32,48,384]{2,1,0:T(8,128)}, ...), condition=%wide.region_3.4_spmd, body=%wide.region_2.3_spmd.sunk | while | flops 151013392 | bytes 5972260 | solution.py:85
  309.1 5.0 collective-permute-done
  321.0 5.0 collective-permute-done
  327.8 2.7 fusion.35
  333.0 7.3 collective-permute-done
  342.0 2.7 fusion.35
  344.9 10.9 %collective-permute-done = bf16[48,4096]{1,0:T(8,128)(2,1)} collective-permute-done((bf16[48,4096]{1,0:T(8,128)(2,1)}, bf16[48,4096]{1,0:T(8,128)(2,1)}, u32[]{:S(2)}, u32[]{:S(2)}) %collective-permute-start) | collective-permute-done | bytes 393248 | tf_op jit(solution)/shard_map/while/body/eval_jaxpr/ppermute | solution.py:13
  357.6 2.7 fusion.35
  360.2 11.1 %collective-permute-done = bf16[48,4096]{1,0:T(8,128)(2,1)} collective-permute-done((bf16[48,4096]{1,0:T(8,128)(2,1)}, bf16[48,4096]{1,0:T(8,128)(2,1)}, u32[]{:S(2)}, u32[]{:S(2)}) %collective-permute-start) | collective-permute-done | bytes 393248 | tf_op jit(solution)/shard_map/while/body/eval_jaxpr/ppermute | solution.py:13
  375.8 11.1 %collective-permute-done = bf16[48,4096]{1,0:T(8,128)(2,1)} collective-permute-done((bf16[48,4096]{1,0:T(8,128)(2,1)}, bf16[48,4096]{1,0:T(8,128)(2,1)}, u32[]{:S(2)}, u32[]{:S(2)}) %collective-permute-start) | collective-permute-done | bytes 393248 | tf_op jit(solution)/shard_map/while/body/eval_jaxpr/ppermute | solution.py:13
  388.7 2.7 fusion.35
  391.3 11.1 %collective-permute-done = bf16[48,4096]{1,0:T(8,128)(2,1)} collective-permute-done((bf16[48,4096]{1,0:T(8,128)(2,1)}, bf16[48,4096]{1,0:T(8,128)(2,1)}, u32[]{:S(2)}, u32[]{:S(2)}) %collective-permute-start) | collective-permute-done | bytes 393248 | tf_op jit(solution)/shard_map/while/body/eval_jaxpr/ppermute | solution.py:13
  404.2 2.7 fusion.35
  406.9 11.1 %collective-permute-done = bf16[48,4096]{1,0:T(8,128)(2,1)} collective-permute-done((bf16[48,4096]{1,0:T(8,128)(2,1)}, bf16[48,4096]{1,0:T(8,128)(2,1)}, u32[]{:S(2)}, u32[]{:S(2)}) %collective-permute-start) | collective-permute-done | bytes 393248 | tf_op jit(solution)/shard_map/while/body/eval_jaxpr/ppermute | solution.py:13
  419.8 2.7 fusion.35
  422.5 11.1 %collective-permute-done = bf16[48,4096]{1,0:T(8,128)(2,1)} collective-permute-done((bf16[48,4096]{1,0:T(8,128)(2,1)}, bf16[48,4096]{1,0:T(8,128)(2,1)}, u32[]{:S(2)}, u32[]{:S(2)}) %collective-permute-start) | collective-permute-done | bytes 393248 | tf_op jit(solution)/shard_map/while/body/eval_jaxpr/ppermute | solution.py:13
  438.0 11.1 %collective-permute-done = bf16[48,4096]{1,0:T(8,128)(2,1)} collective-permute-done((bf16[48,4096]{1,0:T(8,128)(2,1)}, bf16[48,4096]{1,0:T(8,128)(2,1)}, u32[]{:S(2)}, u32[]{:S(2)}) %collective-permute-start) | collective-permute-done | bytes 393248 | tf_op jit(solution)/shard_map/while/body/eval_jaxpr/ppermute | solution.py:13
  450.9 2.7 fusion.35
  453.6 11.1 %collective-permute-done = bf16[48,4096]{1,0:T(8,128)(2,1)} collective-permute-done((bf16[48,4096]{1,0:T(8,128)(2,1)}, bf16[48,4096]{1,0:T(8,128)(2,1)}, u32[]{:S(2)}, u32[]{:S(2)}) %collective-permute-start) | collective-permute-done | bytes 393248 | tf_op jit(solution)/shard_map/while/body/eval_jaxpr/ppermute | solution.py:13
  466.5 2.7 fusion.35
  469.1 11.1 %collective-permute-done = bf16[48,4096]{1,0:T(8,128)(2,1)} collective-permute-done((bf16[48,4096]{1,0:T(8,128)(2,1)}, bf16[48,4096]{1,0:T(8,128)(2,1)}, u32[]{:S(2)}, u32[]{:S(2)}) %collective-permute-start) | collective-permute-done | bytes 393248 | tf_op jit(solution)/shard_map/while/body/eval_jaxpr/ppermute | solution.py:13
  482.0 2.7 fusion.35
  484.7 11.1 %collective-permute-done = bf16[48,4096]{1,0:T(8,128)(2,1)} collective-permute-done((bf16[48,4096]{1,0:T(8,128)(2,1)}, bf16[48,4096]{1,0:T(8,128)(2,1)}, u32[]{:S(2)}, u32[]{:S(2)}) %collective-permute-start) | collective-permute-done | bytes 393248 | tf_op jit(solution)/shard_map/while/body/eval_jaxpr/ppermute | solution.py:13
  500.3 11.1 %collective-permute-done = bf16[48,4096]{1,0:T(8,128)(2,1)} collective-permute-done((bf16[48,4096]{1,0:T(8,128)(2,1)}, bf16[48,4096]{1,0:T(8,128)(2,1)}, u32[]{:S(2)}, u32[]{:S(2)}) %collective-permute-start) | collective-permute-done | bytes 393248 | tf_op jit(solution)/shard_map/while/body/eval_jaxpr/ppermute | solution.py:13
  513.2 2.7 fusion.35
  515.8 11.1 %collective-permute-done = bf16[48,4096]{1,0:T(8,128)(2,1)} collective-permute-done((bf16[48,4096]{1,0:T(8,128)(2,1)}, bf16[48,4096]{1,0:T(8,128)(2,1)}, u32[]{:S(2)}, u32[]{:S(2)}) %collective-permute-start) | collective-permute-done | bytes 393248 | tf_op jit(solution)/shard_map/while/body/eval_jaxpr/ppermute | solution.py:13
  528.7 2.7 fusion.35
  531.4 11.1 %collective-permute-done = bf16[48,4096]{1,0:T(8,128)(2,1)} collective-permute-done((bf16[48,4096]{1,0:T(8,128)(2,1)}, bf16[48,4096]{1,0:T(8,128)(2,1)}, u32[]{:S(2)}, u32[]{:S(2)}) %collective-permute-start) | collective-permute-done | bytes 393248 | tf_op jit(solution)/shard_map/while/body/eval_jaxpr/ppermute | solution.py:13
  544.3 2.7 fusion.35
  546.9 11.1 %collective-permute-done = bf16[48,4096]{1,0:T(8,128)(2,1)} collective-permute-done((bf16[48,4096]{1,0:T(8,128)(2,1)}, bf16[48,4096]{1,0:T(8,128)(2,1)}, u32[]{:S(2)}, u32[]{:S(2)}) %collective-permute-start) | collective-permute-done | bytes 393248 | tf_op jit(solution)/shard_map/while/body/eval_jaxpr/ppermute | solution.py:13
  562.5 11.1 %collective-permute-done = bf16[48,4096]{1,0:T(8,128)(2,1)} collective-permute-done((bf16[48,4096]{1,0:T(8,128)(2,1)}, bf16[48,4096]{1,0:T(8,128)(2,1)}, u32[]{:S(2)}, u32[]{:S(2)}) %collective-permute-start) | collective-permute-done | bytes 393248 | tf_op jit(solution)/shard_map/while/body/eval_jaxpr/ppermute | solution.py:13
  575.4 2.7 fusion.35
  578.1 11.1 %collective-permute-done = bf16[48,4096]{1,0:T(8,128)(2,1)} collective-permute-done((bf16[48,4096]{1,0:T(8,128)(2,1)}, bf16[48,4096]{1,0:T(8,128)(2,1)}, u32[]{:S(2)}, u32[]{:S(2)}) %collective-permute-start) | collective-permute-done | bytes 393248 | tf_op jit(solution)/shard_map/while/body/eval_jaxpr/ppermute | solution.py:13
  591.0 2.7 fusion.35
  593.6 11.1 %collective-permute-done = bf16[48,4096]{1,0:T(8,128)(2,1)} collective-permute-done((bf16[48,4096]{1,0:T(8,128)(2,1)}, bf16[48,4096]{1,0:T(8,128)(2,1)}, u32[]{:S(2)}, u32[]{:S(2)}) %collective-permute-start) | collective-permute-done | bytes 393248 | tf_op jit(solution)/shard_map/while/body/eval_jaxpr/ppermute | solution.py:13
  606.5 2.7 fusion.35
  609.2 11.1 %collective-permute-done = bf16[48,4096]{1,0:T(8,128)(2,1)} collective-permute-done((bf16[48,4096]{1,0:T(8,128)(2,1)}, bf16[48,4096]{1,0:T(8,128)(2,1)}, u32[]{:S(2)}, u32[]{:S(2)}) %collective-permute-start) | collective-permute-done | bytes 393248 | tf_op jit(solution)/shard_map/while/body/eval_jaxpr/ppermute | solution.py:13
  624.7 11.1 %collective-permute-done = bf16[48,4096]{1,0:T(8,128)(2,1)} collective-permute-done((bf16[48,4096]{1,0:T(8,128)(2,1)}, bf16[48,4096]{1,0:T(8,128)(2,1)}, u32[]{:S(2)}, u32[]{:S(2)}) %collective-permute-start) | collective-permute-done | bytes 393248 | tf_op jit(solution)/shard_map/while/body/eval_jaxpr/ppermute | solution.py:13
  637.6 2.7 fusion.35
  640.3 11.1 %collective-permute-done = bf16[48,4096]{1,0:T(8,128)(2,1)} collective-permute-done((bf16[48,4096]{1,0:T(8,128)(2,1)}, bf16[48,4096]{1,0:T(8,128)(2,1)}, u32[]{:S(2)}, u32[]{:S(2)}) %collective-permute-start) | collective-permute-done | bytes 393248 | tf_op jit(solution)/shard_map/while/body/eval_jaxpr/ppermute | solution.py:13
  653.2 2.7 fusion.35
  655.9 11.1 %collective-permute-done = bf16[48,4096]{1,0:T(8,128)(2,1)} collective-permute-done((bf16[48,4096]{1,0:T(8,128)(2,1)}, bf16[48,4096]{1,0:T(8,128)(2,1)}, u32[]{:S(2)}, u32[]{:S(2)}) %collective-permute-start) | collective-permute-done | bytes 393248 | tf_op jit(solution)/shard_map/while/body/eval_jaxpr/ppermute | solution.py:13
  668.8 2.7 fusion.35
  671.4 11.1 %collective-permute-done = bf16[48,4096]{1,0:T(8,128)(2,1)} collective-permute-done((bf16[48,4096]{1,0:T(8,128)(2,1)}, bf16[48,4096]{1,0:T(8,128)(2,1)}, u32[]{:S(2)}, u32[]{:S(2)}) %collective-permute-start) | collective-permute-done | bytes 393248 | tf_op jit(solution)/shard_map/while/body/eval_jaxpr/ppermute | solution.py:13
  687.0 11.1 %collective-permute-done = bf16[48,4096]{1,0:T(8,128)(2,1)} collective-permute-done((bf16[48,4096]{1,0:T(8,128)(2,1)}, bf16[48,4096]{1,0:T(8,128)(2,1)}, u32[]{:S(2)}, u32[]{:S(2)}) %collective-permute-start) | collective-permute-done | bytes 393248 | tf_op jit(solution)/shard_map/while/body/eval_jaxpr/ppermute | solution.py:13
  699.9 2.7 fusion.35
  702.5 11.1 %collective-permute-done = bf16[48,4096]{1,0:T(8,128)(2,1)} collective-permute-done((bf16[48,4096]{1,0:T(8,128)(2,1)}, bf16[48,4096]{1,0:T(8,128)(2,1)}, u32[]{:S(2)}, u32[]{:S(2)}) %collective-permute-start) | collective-permute-done | bytes 393248 | tf_op jit(solution)/shard_map/while/body/eval_jaxpr/ppermute | solution.py:13
  715.4 2.7 fusion.35
  718.1 11.1 %collective-permute-done = bf16[48,4096]{1,0:T(8,128)(2,1)} collective-permute-done((bf16[48,4096]{1,0:T(8,128)(2,1)}, bf16[48,4096]{1,0:T(8,128)(2,1)}, u32[]{:S(2)}, u32[]{:S(2)}) %collective-permute-start) | collective-permute-done | bytes 393248 | tf_op jit(solution)/shard_map/while/body/eval_jaxpr/ppermute | solution.py:13
  731.0 2.7 fusion.35
  733.7 11.1 %collective-permute-done = bf16[48,4096]{1,0:T(8,128)(2,1)} collective-permute-done((bf16[48,4096]{1,0:T(8,128)(2,1)}, bf16[48,4096]{1,0:T(8,128)(2,1)}, u32[]{:S(2)}, u32[]{:S(2)}) %collective-permute-start) | collective-permute-done | bytes 393248 | tf_op jit(solution)/shard_map/while/body/eval_jaxpr/ppermute | solution.py:13
  749.2 11.1 %collective-permute-done = bf16[48,4096]{1,0:T(8,128)(2,1)} collective-permute-done((bf16[48,4096]{1,0:T(8,128)(2,1)}, bf16[48,4096]{1,0:T(8,128)(2,1)}, u32[]{:S(2)}, u32[]{:S(2)}) %collective-permute-start) | collective-permute-done | bytes 393248 | tf_op jit(solution)/shard_map/while/body/eval_jaxpr/ppermute | solution.py:13
  762.1 2.7 fusion.35
  764.8 11.1 %collective-permute-done = bf16[48,4096]{1,0:T(8,128)(2,1)} collective-permute-done((bf16[48,4096]{1,0:T(8,128)(2,1)}, bf16[48,4096]{1,0:T(8,128)(2,1)}, u32[]{:S(2)}, u32[]{:S(2)}) %collective-permute-start) | collective-permute-done | bytes 393248 | tf_op jit(solution)/shard_map/while/body/eval_jaxpr/ppermute | solution.py:13
  777.7 2.7 fusion.35
  (93 shorter events, 90.4 us)
Async XLA Ops:
  7.2 55.6 %copy-start = (bf16[4,128,128]{2,1,0:T(8,128)(2,1)S(1)}, bf16[4,128,128]{2,1,0:T(8,128)(2,1)}, u32[]{:S(2)}) copy-start(bf16[4,128,128]{2,1,0:T(8,128)(2,1)} %param.9) | copy-start | bytes 393220
  7.2 0.8 copy-start.5
  7.2 55.6 %reduce-scatter.3.cloned.1.call-start = ((), (), s32[]{:S(2)}) async-start(), calls=%async_computation.2 | async-start | bytes 4718592 | tf_op jit(solution)/shard_map/reduce_scatter | solution.py:47
  7.9 218.1 %reduce-scatter.5.cloned.1.call-start = ((), (), s32[]{:S(2)}) async-start(), calls=%async_computation.3 | async-start | bytes 7077888 | tf_op jit(solution)/shard_map/reduce_scatter | solution.py:56
  62.8 3.3 copy-start.3
  72.0 7.2 copy-start.2
  92.6 209.6 %all-gather.2.cloned.1.call-start = ((), (), s32[]{:S(2)}) async-start(), calls=%async_computation.4 | async-start | bytes 3538944 | tf_op jit(solution)/shard_map/all_gather | solution.py:58
  302.1 4.8 copy-start.1
  305.5 1.4 copy-start.4
  306.9 7.2 collective-permute-start
  318.5 7.5 collective-permute-start
  330.5 9.7 %collective-permute-start = (bf16[48,4096]{1,0:T(8,128)(2,1)}, bf16[48,4096]{1,0:T(8,128)(2,1)}, u32[]{:S(2)}, u32[]{:S(2)}) collective-permute-start(bf16[48,4096]{1,0:T(8,128)(2,1)} %get-tuple-element.189), channel_id=1, source_target_pairs={{0,8},{8,16},{16,24},{24,32},{32,40},{40,48},{48,56},{56,64},{64,7... | collective-permute-start | bytes 1179656 | tf_op jit(solution)/shard_map/while/body/eval_jaxpr/ppermute | solution.py:13
  344.7 11.1 %collective-permute-start = (bf16[48,4096]{1,0:T(8,128)(2,1)}, bf16[48,4096]{1,0:T(8,128)(2,1)}, u32[]{:S(2)}, u32[]{:S(2)}) collective-permute-start(bf16[48,4096]{1,0:T(8,128)(2,1)} %get-tuple-element.189), channel_id=1, source_target_pairs={{0,8},{8,16},{16,24},{24,32},{32,40},{40,48},{48,56},{56,64},{64,7... | collective-permute-start | bytes 1179656 | tf_op jit(solution)/shard_map/while/body/eval_jaxpr/ppermute | solution.py:13
  360.2 11.1 %collective-permute-start = (bf16[48,4096]{1,0:T(8,128)(2,1)}, bf16[48,4096]{1,0:T(8,128)(2,1)}, u32[]{:S(2)}, u32[]{:S(2)}) collective-permute-start(bf16[48,4096]{1,0:T(8,128)(2,1)} %get-tuple-element.189), channel_id=1, source_target_pairs={{0,8},{8,16},{16,24},{24,32},{32,40},{40,48},{48,56},{56,64},{64,7... | collective-permute-start | bytes 1179656 | tf_op jit(solution)/shard_map/while/body/eval_jaxpr/ppermute | solution.py:13
  375.8 11.1 %collective-permute-start = (bf16[48,4096]{1,0:T(8,128)(2,1)}, bf16[48,4096]{1,0:T(8,128)(2,1)}, u32[]{:S(2)}, u32[]{:S(2)}) collective-permute-start(bf16[48,4096]{1,0:T(8,128)(2,1)} %get-tuple-element.189), channel_id=1, source_target_pairs={{0,8},{8,16},{16,24},{24,32},{32,40},{40,48},{48,56},{56,64},{64,7... | collective-permute-start | bytes 1179656 | tf_op jit(solution)/shard_map/while/body/eval_jaxpr/ppermute | solution.py:13
  391.3 11.1 %collective-permute-start = (bf16[48,4096]{1,0:T(8,128)(2,1)}, bf16[48,4096]{1,0:T(8,128)(2,1)}, u32[]{:S(2)}, u32[]{:S(2)}) collective-permute-start(bf16[48,4096]{1,0:T(8,128)(2,1)} %get-tuple-element.189), channel_id=1, source_target_pairs={{0,8},{8,16},{16,24},{24,32},{32,40},{40,48},{48,56},{56,64},{64,7... | collective-permute-start | bytes 1179656 | tf_op jit(solution)/shard_map/while/body/eval_jaxpr/ppermute | solution.py:13
  406.9 11.1 %collective-permute-start = (bf16[48,4096]{1,0:T(8,128)(2,1)}, bf16[48,4096]{1,0:T(8,128)(2,1)}, u32[]{:S(2)}, u32[]{:S(2)}) collective-permute-start(bf16[48,4096]{1,0:T(8,128)(2,1)} %get-tuple-element.189), channel_id=1, source_target_pairs={{0,8},{8,16},{16,24},{24,32},{32,40},{40,48},{48,56},{56,64},{64,7... | collective-permute-start | bytes 1179656 | tf_op jit(solution)/shard_map/while/body/eval_jaxpr/ppermute | solution.py:13
  422.5 11.1 %collective-permute-start = (bf16[48,4096]{1,0:T(8,128)(2,1)}, bf16[48,4096]{1,0:T(8,128)(2,1)}, u32[]{:S(2)}, u32[]{:S(2)}) collective-permute-start(bf16[48,4096]{1,0:T(8,128)(2,1)} %get-tuple-element.189), channel_id=1, source_target_pairs={{0,8},{8,16},{16,24},{24,32},{32,40},{40,48},{48,56},{56,64},{64,7... | collective-permute-start | bytes 1179656 | tf_op jit(solution)/shard_map/while/body/eval_jaxpr/ppermute | solution.py:13
  438.0 11.1 %collective-permute-start = (bf16[48,4096]{1,0:T(8,128)(2,1)}, bf16[48,4096]{1,0:T(8,128)(2,1)}, u32[]{:S(2)}, u32[]{:S(2)}) collective-permute-start(bf16[48,4096]{1,0:T(8,128)(2,1)} %get-tuple-element.189), channel_id=1, source_target_pairs={{0,8},{8,16},{16,24},{24,32},{32,40},{40,48},{48,56},{56,64},{64,7... | collective-permute-start | bytes 1179656 | tf_op jit(solution)/shard_map/while/body/eval_jaxpr/ppermute | solution.py:13
  453.6 11.1 %collective-permute-start = (bf16[48,4096]{1,0:T(8,128)(2,1)}, bf16[48,4096]{1,0:T(8,128)(2,1)}, u32[]{:S(2)}, u32[]{:S(2)}) collective-permute-start(bf16[48,4096]{1,0:T(8,128)(2,1)} %get-tuple-element.189), channel_id=1, source_target_pairs={{0,8},{8,16},{16,24},{24,32},{32,40},{40,48},{48,56},{56,64},{64,7... | collective-permute-start | bytes 1179656 | tf_op jit(solution)/shard_map/while/body/eval_jaxpr/ppermute | solution.py:13
  469.1 11.1 %collective-permute-start = (bf16[48,4096]{1,0:T(8,128)(2,1)}, bf16[48,4096]{1,0:T(8,128)(2,1)}, u32[]{:S(2)}, u32[]{:S(2)}) collective-permute-start(bf16[48,4096]{1,0:T(8,128)(2,1)} %get-tuple-element.189), channel_id=1, source_target_pairs={{0,8},{8,16},{16,24},{24,32},{32,40},{40,48},{48,56},{56,64},{64,7... | collective-permute-start | bytes 1179656 | tf_op jit(solution)/shard_map/while/body/eval_jaxpr/ppermute | solution.py:13
  484.7 11.1 %collective-permute-start = (bf16[48,4096]{1,0:T(8,128)(2,1)}, bf16[48,4096]{1,0:T(8,128)(2,1)}, u32[]{:S(2)}, u32[]{:S(2)}) collective-permute-start(bf16[48,4096]{1,0:T(8,128)(2,1)} %get-tuple-element.189), channel_id=1, source_target_pairs={{0,8},{8,16},{16,24},{24,32},{32,40},{40,48},{48,56},{56,64},{64,7... | collective-permute-start | bytes 1179656 | tf_op jit(solution)/shard_map/while/body/eval_jaxpr/ppermute | solution.py:13
  500.3 11.1 %collective-permute-start = (bf16[48,4096]{1,0:T(8,128)(2,1)}, bf16[48,4096]{1,0:T(8,128)(2,1)}, u32[]{:S(2)}, u32[]{:S(2)}) collective-permute-start(bf16[48,4096]{1,0:T(8,128)(2,1)} %get-tuple-element.189), channel_id=1, source_target_pairs={{0,8},{8,16},{16,24},{24,32},{32,40},{40,48},{48,56},{56,64},{64,7... | collective-permute-start | bytes 1179656 | tf_op jit(solution)/shard_map/while/body/eval_jaxpr/ppermute | solution.py:13
  515.8 11.1 %collective-permute-start = (bf16[48,4096]{1,0:T(8,128)(2,1)}, bf16[48,4096]{1,0:T(8,128)(2,1)}, u32[]{:S(2)}, u32[]{:S(2)}) collective-permute-start(bf16[48,4096]{1,0:T(8,128)(2,1)} %get-tuple-element.189), channel_id=1, source_target_pairs={{0,8},{8,16},{16,24},{24,32},{32,40},{40,48},{48,56},{56,64},{64,7... | collective-permute-start | bytes 1179656 | tf_op jit(solution)/shard_map/while/body/eval_jaxpr/ppermute | solution.py:13
  531.4 11.1 %collective-permute-start = (bf16[48,4096]{1,0:T(8,128)(2,1)}, bf16[48,4096]{1,0:T(8,128)(2,1)}, u32[]{:S(2)}, u32[]{:S(2)}) collective-permute-start(bf16[48,4096]{1,0:T(8,128)(2,1)} %get-tuple-element.189), channel_id=1, source_target_pairs={{0,8},{8,16},{16,24},{24,32},{32,40},{40,48},{48,56},{56,64},{64,7... | collective-permute-start | bytes 1179656 | tf_op jit(solution)/shard_map/while/body/eval_jaxpr/ppermute | solution.py:13
  546.9 11.1 %collective-permute-start = (bf16[48,4096]{1,0:T(8,128)(2,1)}, bf16[48,4096]{1,0:T(8,128)(2,1)}, u32[]{:S(2)}, u32[]{:S(2)}) collective-permute-start(bf16[48,4096]{1,0:T(8,128)(2,1)} %get-tuple-element.189), channel_id=1, source_target_pairs={{0,8},{8,16},{16,24},{24,32},{32,40},{40,48},{48,56},{56,64},{64,7... | collective-permute-start | bytes 1179656 | tf_op jit(solution)/shard_map/while/body/eval_jaxpr/ppermute | solution.py:13
  562.5 11.1 %collective-permute-start = (bf16[48,4096]{1,0:T(8,128)(2,1)}, bf16[48,4096]{1,0:T(8,128)(2,1)}, u32[]{:S(2)}, u32[]{:S(2)}) collective-permute-start(bf16[48,4096]{1,0:T(8,128)(2,1)} %get-tuple-element.189), channel_id=1, source_target_pairs={{0,8},{8,16},{16,24},{24,32},{32,40},{40,48},{48,56},{56,64},{64,7... | collective-permute-start | bytes 1179656 | tf_op jit(solution)/shard_map/while/body/eval_jaxpr/ppermute | solution.py:13
  578.1 11.1 %collective-permute-start = (bf16[48,4096]{1,0:T(8,128)(2,1)}, bf16[48,4096]{1,0:T(8,128)(2,1)}, u32[]{:S(2)}, u32[]{:S(2)}) collective-permute-start(bf16[48,4096]{1,0:T(8,128)(2,1)} %get-tuple-element.189), channel_id=1, source_target_pairs={{0,8},{8,16},{16,24},{24,32},{32,40},{40,48},{48,56},{56,64},{64,7... | collective-permute-start | bytes 1179656 | tf_op jit(solution)/shard_map/while/body/eval_jaxpr/ppermute | solution.py:13
  593.6 11.1 %collective-permute-start = (bf16[48,4096]{1,0:T(8,128)(2,1)}, bf16[48,4096]{1,0:T(8,128)(2,1)}, u32[]{:S(2)}, u32[]{:S(2)}) collective-permute-start(bf16[48,4096]{1,0:T(8,128)(2,1)} %get-tuple-element.189), channel_id=1, source_target_pairs={{0,8},{8,16},{16,24},{24,32},{32,40},{40,48},{48,56},{56,64},{64,7... | collective-permute-start | bytes 1179656 | tf_op jit(solution)/shard_map/while/body/eval_jaxpr/ppermute | solution.py:13
  609.2 11.1 %collective-permute-start = (bf16[48,4096]{1,0:T(8,128)(2,1)}, bf16[48,4096]{1,0:T(8,128)(2,1)}, u32[]{:S(2)}, u32[]{:S(2)}) collective-permute-start(bf16[48,4096]{1,0:T(8,128)(2,1)} %get-tuple-element.189), channel_id=1, source_target_pairs={{0,8},{8,16},{16,24},{24,32},{32,40},{40,48},{48,56},{56,64},{64,7... | collective-permute-start | bytes 1179656 | tf_op jit(solution)/shard_map/while/body/eval_jaxpr/ppermute | solution.py:13
  624.7 11.1 %collective-permute-start = (bf16[48,4096]{1,0:T(8,128)(2,1)}, bf16[48,4096]{1,0:T(8,128)(2,1)}, u32[]{:S(2)}, u32[]{:S(2)}) collective-permute-start(bf16[48,4096]{1,0:T(8,128)(2,1)} %get-tuple-element.189), channel_id=1, source_target_pairs={{0,8},{8,16},{16,24},{24,32},{32,40},{40,48},{48,56},{56,64},{64,7... | collective-permute-start | bytes 1179656 | tf_op jit(solution)/shard_map/while/body/eval_jaxpr/ppermute | solution.py:13
  640.3 11.1 %collective-permute-start = (bf16[48,4096]{1,0:T(8,128)(2,1)}, bf16[48,4096]{1,0:T(8,128)(2,1)}, u32[]{:S(2)}, u32[]{:S(2)}) collective-permute-start(bf16[48,4096]{1,0:T(8,128)(2,1)} %get-tuple-element.189), channel_id=1, source_target_pairs={{0,8},{8,16},{16,24},{24,32},{32,40},{40,48},{48,56},{56,64},{64,7... | collective-permute-start | bytes 1179656 | tf_op jit(solution)/shard_map/while/body/eval_jaxpr/ppermute | solution.py:13
  655.9 11.1 %collective-permute-start = (bf16[48,4096]{1,0:T(8,128)(2,1)}, bf16[48,4096]{1,0:T(8,128)(2,1)}, u32[]{:S(2)}, u32[]{:S(2)}) collective-permute-start(bf16[48,4096]{1,0:T(8,128)(2,1)} %get-tuple-element.189), channel_id=1, source_target_pairs={{0,8},{8,16},{16,24},{24,32},{32,40},{40,48},{48,56},{56,64},{64,7... | collective-permute-start | bytes 1179656 | tf_op jit(solution)/shard_map/while/body/eval_jaxpr/ppermute | solution.py:13
  671.4 11.1 %collective-permute-start = (bf16[48,4096]{1,0:T(8,128)(2,1)}, bf16[48,4096]{1,0:T(8,128)(2,1)}, u32[]{:S(2)}, u32[]{:S(2)}) collective-permute-start(bf16[48,4096]{1,0:T(8,128)(2,1)} %get-tuple-element.189), channel_id=1, source_target_pairs={{0,8},{8,16},{16,24},{24,32},{32,40},{40,48},{48,56},{56,64},{64,7... | collective-permute-start | bytes 1179656 | tf_op jit(solution)/shard_map/while/body/eval_jaxpr/ppermute | solution.py:13
  687.0 11.1 %collective-permute-start = (bf16[48,4096]{1,0:T(8,128)(2,1)}, bf16[48,4096]{1,0:T(8,128)(2,1)}, u32[]{:S(2)}, u32[]{:S(2)}) collective-permute-start(bf16[48,4096]{1,0:T(8,128)(2,1)} %get-tuple-element.189), channel_id=1, source_target_pairs={{0,8},{8,16},{16,24},{24,32},{32,40},{40,48},{48,56},{56,64},{64,7... | collective-permute-start | bytes 1179656 | tf_op jit(solution)/shard_map/while/body/eval_jaxpr/ppermute | solution.py:13
  702.5 11.1 %collective-permute-start = (bf16[48,4096]{1,0:T(8,128)(2,1)}, bf16[48,4096]{1,0:T(8,128)(2,1)}, u32[]{:S(2)}, u32[]{:S(2)}) collective-permute-start(bf16[48,4096]{1,0:T(8,128)(2,1)} %get-tuple-element.189), channel_id=1, source_target_pairs={{0,8},{8,16},{16,24},{24,32},{32,40},{40,48},{48,56},{56,64},{64,7... | collective-permute-start | bytes 1179656 | tf_op jit(solution)/shard_map/while/body/eval_jaxpr/ppermute | solution.py:13
  718.1 11.1 %collective-permute-start = (bf16[48,4096]{1,0:T(8,128)(2,1)}, bf16[48,4096]{1,0:T(8,128)(2,1)}, u32[]{:S(2)}, u32[]{:S(2)}) collective-permute-start(bf16[48,4096]{1,0:T(8,128)(2,1)} %get-tuple-element.189), channel_id=1, source_target_pairs={{0,8},{8,16},{16,24},{24,32},{32,40},{40,48},{48,56},{56,64},{64,7... | collective-permute-start | bytes 1179656 | tf_op jit(solution)/shard_map/while/body/eval_jaxpr/ppermute | solution.py:13
  733.7 11.1 %collective-permute-start = (bf16[48,4096]{1,0:T(8,128)(2,1)}, bf16[48,4096]{1,0:T(8,128)(2,1)}, u32[]{:S(2)}, u32[]{:S(2)}) collective-permute-start(bf16[48,4096]{1,0:T(8,128)(2,1)} %get-tuple-element.189), channel_id=1, source_target_pairs={{0,8},{8,16},{16,24},{24,32},{32,40},{40,48},{48,56},{56,64},{64,7... | collective-permute-start | bytes 1179656 | tf_op jit(solution)/shard_map/while/body/eval_jaxpr/ppermute | solution.py:13
  749.2 11.1 %collective-permute-start = (bf16[48,4096]{1,0:T(8,128)(2,1)}, bf16[48,4096]{1,0:T(8,128)(2,1)}, u32[]{:S(2)}, u32[]{:S(2)}) collective-permute-start(bf16[48,4096]{1,0:T(8,128)(2,1)} %get-tuple-element.189), channel_id=1, source_target_pairs={{0,8},{8,16},{16,24},{24,32},{32,40},{40,48},{48,56},{56,64},{64,7... | collective-permute-start | bytes 1179656 | tf_op jit(solution)/shard_map/while/body/eval_jaxpr/ppermute | solution.py:13
  764.8 11.1 %collective-permute-start = (bf16[48,4096]{1,0:T(8,128)(2,1)}, bf16[48,4096]{1,0:T(8,128)(2,1)}, u32[]{:S(2)}, u32[]{:S(2)}) collective-permute-start(bf16[48,4096]{1,0:T(8,128)(2,1)} %get-tuple-element.189), channel_id=1, source_target_pairs={{0,8},{8,16},{16,24},{24,32},{32,40},{40,48},{48,56},{56,64},{64,7... | collective-permute-start | bytes 1179656 | tf_op jit(solution)/shard_map/while/body/eval_jaxpr/ppermute | solution.py:13
Sparse Core Ops, SparseCore 0:
  10.5 52.2 reduce-scatter.2
  92.7 133.2 reduce-scatter.4
  228.5 73.5 all-gather.1
where the time goes:
time: 799 us; the launch traced here: 787 us
  waiting for transfers between devices  589 us (74%)
  matrix products  107 us (13%)
  local copies, waits for them, and re-layouts  67 us (8%)
  between operations  13.9 us (2%)
    ppermute x31, waiting for transfers between devices, shifted(): return lax.ppermute(value, axis, pairs)  329 us
    reduce_scatter x1, waiting for transfers between devices, on_device(): lax.psum_scatter(partial_sketch, ('shard', 'tensor'), scatter_dimension=0...  133 us
    dot_general x32, matrix products, tile_block(): lax.dot_general(moving, row_sketch, (((1,), (1,)), ((), ())), preferred_e...  85.7 us
    all_gather x1, waiting for transfers between devices, on_device(): lax.all_gather(own_sketch, ('shard', 'tensor'), axis=0, tiled=True)  72.4 us
    while x31, local copies, waits for them, and re-layouts  54.7 us
    reduce_scatter x1, waiting for transfers between devices, on_device(): lax.psum_scatter(own_rows.astype(jnp.float32).astype(jnp.bfloat16), 'tens...  54 us
  transfers between devices with their start and end apart: 34, of which 34 were waited for; matrix products, arithmetic and copies ran while one was open for 0% of the time, Pallas kernels for 0%

commit v1 on v0

v1 whole, which is shorter than its diff:
```python
import functools

import jax
import jax.numpy as jnp
from jax import lax
from jax.experimental import pallas as pl
from jax.experimental.pallas import tpu as pltpu
from jax.sharding import PartitionSpec as P

SKETCH = 4096
BLOCK = 128
FAN = 4
SB = SKETCH // BLOCK
NX, NT, NZ, NY, NC = 4, 2, 8, 2, 2
PART = 3
ROWS = 16
MESH = pl.DeviceIdType.MESH
F32 = jnp.float32
BF16 = jnp.bfloat16


def split_pair(values):
    upper = values.astype(BF16)
    return upper, (values - upper.astype(F32)).astype(BF16)


def kernel_body(
    x_ref, map_ref, sign_ref, blocks_ref, sketch_ref, out_ref,
    rx, gath, rows, grad, wide, low, onehot, signs, stacked,
    local_sem, a2a_s, a2a_r, sib_s, sib_r, y2_s, y2_r, yp_s, yp_r, x_s, x_r, z_s, z_r,
):
    group = lax.axis_index("group")
    x = lax.axis_index("shard")
    t = lax.axis_index("tensor")
    yh = group // (NZ * NC)
    z = lax.rem(group, NZ * NC) // NC
    c = lax.rem(group, NC)
    d = x * NT + t

    def at_group(yy, zz, cc):
        return {"group": (yy * NZ + zz) * NC + cc}

    sibling = at_group(yh, z, 1 - c)
    across = at_group(1 - yh, z, c)
    ahead = at_group(yh, lax.rem(z + 1, NZ), c)
    behind = at_group(yh, lax.rem(z + NZ - 1, NZ), c)
    z_way = (ahead, behind)

    def member(j):
        e = lax.rem(d + j, NX * NT)
        return e, {"shard": e // NT, "tensor": lax.rem(e, NT)}

    barrier = pltpu.get_barrier_semaphore()
    for target in [member(j)[1] for j in range(1, 8)] + [sibling, across, ahead, behind]:
        pl.semaphore_signal(barrier, inc=1, device_id=target, device_id_type=MESH)
    pl.semaphore_wait(barrier, 11)

    def remote(src, dst, s, r, target):
        return pltpu.make_async_remote_copy(
            src_ref=src, dst_ref=dst, send_sem=s, recv_sem=r, device_id=target, device_id_type=MESH
        )

    started = []

    def start(copy):
        copy.start()
        started.append(copy)
        return copy

    def exchange(i):
        own = pltpu.make_async_copy(
            x_ref.at[pl.ds(pl.multiple_of(d * PART * ROWS + i * ROWS, ROWS), ROWS), :],
            rx.at[i, x, t], local_sem.at[i],
        )
        own.start()
        copies = []
        for j in range(1, 8):
            e, target = member(j)
            src = x_ref.at[pl.ds(pl.multiple_of(e * PART * ROWS + i * ROWS, ROWS), ROWS), :]
            copies.append(start(remote(src, rx.at[i, x, t], a2a_s.at[i, j - 1], a2a_r.at[i, j - 1], target)))
        return own, copies

    def project(i):
        @pl.loop(0, NX)
        def _(xx):
            for b in range(SB):
                lanes = pl.ds(b * BLOCK, BLOCK)
                both = rx[i, xx, 0, :, lanes].astype(F32) + rx[i, xx, 1, :, lanes].astype(F32)
                grad[pl.ds(xx * SB + b, ROWS, stride=NX * SB), :] = both

        @pl.loop(0, ROWS // 2)
        def _(pair):
            parts = []
            for e in range(2):
                signed = grad[pl.ds(pl.multiple_of((pair * 2 + e) * BLOCK, BLOCK), BLOCK), :] * signs[...]
                upper, lower = split_pair(signed)
                parts.append(jnp.concatenate([upper, lower], axis=0))
            summed = jnp.dot(onehot[...], jnp.concatenate(parts, axis=1), preferred_element_type=F32)
            upper, lower = split_pair(summed)
            for e in range(2):
                place = pl.ds(pl.multiple_of((pair * 2 + e) * SB, SB), SB)
                cols = slice(e * BLOCK, (e + 1) * BLOCK)
                for f in range(FAN):
                    fr = slice(f * SB, (f + 1) * SB)
                    wide[place, f * BLOCK:(f + 1) * BLOCK] = upper[fr, cols]
                    wide[place, (FAN + f) * BLOCK:(FAN + f + 1) * BLOCK] = lower[fr, cols]

        low[...] = jnp.dot(wide[...], stacked[...], preferred_element_type=F32)
        for s in range(SB):
            piece = low[pl.ds(s, ROWS, stride=SB), :].astype(BF16)
            lanes = slice(s * BLOCK, (s + 1) * BLOCK)
            gath[z, c, yh, i, :, lanes] = piece
            rows[x, t, i, :, lanes] = piece
            sketch_ref[i * ROWS:(i + 1) * ROWS, lanes] = piece

    def spread(i):
        own = gath.at[z, c, yh, i]
        zc = [start(remote(own, own, z_s.at[i, w, 0], z_r.at[i, w, 0], z_way[w])) for w in range(2)]
        y2 = start(remote(own, own, y2_s.at[i], y2_r.at[i], across))
        mine = rows.at[x, t, i]
        yp = start(remote(mine, mine, yp_s.at[i], yp_r.at[i], {"tensor": 1 - t}))
        sb = start(remote(own, own, sib_s.at[i, 0], sib_r.at[i, 0], sibling))
        return zc, y2, yp, sb

    def along_x(i, k, tt):
        block = rows.at[x, tt, i]
        return [
            start(remote(block, block, x_s.at[i, k, j - 1], x_r.at[i, k, j - 1], {"shard": lax.rem(x + j, NX)}))
            for j in (1, 3, 2)
        ]

    def relay_across(i):
        other = gath.at[z, c, 1 - yh, i]
        zc = [start(remote(other, other, z_s.at[i, w, 1], z_r.at[i, w, 1], z_way[w])) for w in range(2)]
        sb = start(remote(other, other, sib_s.at[i, 1], sib_r.at[i, 1], sibling))
        return zc, sb

    def z_block(w, h, i, both, k=None):
        zz = lax.rem(z + NZ - h, NZ) if w == 0 else lax.rem(z + h, NZ)
        return gath.at[zz, c, :, i] if both else gath.at[zz, c, k, i]

    def z_step(i, h, arriving):
        out, sbs = [], []
        for w in range(2):
            for copy in arriving[w]:
                copy.wait_recv()
            if h < 3:
                block = z_block(w, h, i, True)
                out.append([start(remote(block, block, z_s.at[i, w, h + 1], z_r.at[i, w, h + 1], z_way[w]))])
            elif h == 3:
                block = z_block(w, h, i, False, yh if w == 0 else 1 - yh)
                out.append([start(remote(block, block, z_s.at[i, w, 4], z_r.at[i, w, 4], z_way[w]))])
            block = z_block(w, h, i, True) if h < 4 else z_block(w, h, i, False, yh if w == 0 else 1 - yh)
            sbs.append(start(remote(block, block, sib_s.at[i, 1 + w * 4 + h], sib_r.at[i, 1 + w * 4 + h], sibling)))
        return out, sbs

    exchanges = [exchange(0)]

    targets = lax.broadcasted_iota(jnp.int32, (SB, BLOCK), 0)
    for f in range(FAN):
        hot = jnp.where(map_ref[f:f + 1, :] == targets, 1.0, 0.0).astype(BF16)
        onehot[f * SB:(f + 1) * SB, :BLOCK] = hot
        onehot[f * SB:(f + 1) * SB, BLOCK:] = hot
    signs[...] = (2 * sign_ref[...] - 1).astype(F32)
    for f in range(FAN):
        stacked[f * BLOCK:(f + 1) * BLOCK, :] = blocks_ref[f]
        stacked[(FAN + f) * BLOCK:(FAN + f + 1) * BLOCK, :] = blocks_ref[f]

    arrive_z = {}
    arrive_row = []
    arrive_sib = []

    def first(i):
        own, copies = exchanges[i]
        own.wait()
        for copy in copies:
            copy.wait_recv()
        if i + 1 < PART:
            exchanges.append(exchange(i + 1))
        project(i)
        zc, y2, yp, sb = spread(i)
        arrive_row.extend(along_x(i, 0, t))
        y2.wait_recv()
        zc2, sb2 = relay_across(i)
        yp.wait_recv()
        arrive_row.extend(along_x(i, 1, 1 - t))
        arrive_sib.extend([sb, sb2])
        arrive_z[i, 1] = [[zc[w], zc2[w]] for w in range(2)]

    def hop(i, h):
        out, sbs = z_step(i, h, arrive_z[i, h])
        arrive_sib.extend(sbs)
        if out:
            arrive_z[i, h + 1] = out

    first(0)
    hop(0, 1)
    hop(0, 2)
    first(1)
    hop(0, 3)
    hop(1, 1)
    hop(0, 4)
    hop(1, 2)
    first(2)
    hop(1, 3)
    hop(2, 1)
    hop(1, 4)
    hop(2, 2)
    hop(2, 3)
    hop(2, 4)
    for copy in arrive_row:
        copy.wait_recv()
    for copy in arrive_sib:
        copy.wait_recv()

    @pl.loop(0, NZ // 2)
    def _(q):
        left = gath[pl.ds(q * 2, 2)].reshape(2 * NC * NY * PART * ROWS, SKETCH)
        right = rows[...].reshape(NX * NT * PART * ROWS, SKETCH)
        tile = lax.dot_general(left, right, (((1,), (1,)), ((), ())), preferred_element_type=F32) * (1.0 / SKETCH)
        tile = tile.reshape(2, NC, NY, PART * ROWS, NX * NT * PART * ROWS)
        for a in range(2):
            for cc in range(NC):
                for yy in range(NY):
                    out_ref[yy, q * 2 + a, cc] = tile[a, cc, yy]

    for copy in started:
        copy.wait_send()


def on_device(partials, index_map, sign_bits, blocks):
    count = NX * NT * PART * ROWS
    piece = (ROWS, SKETCH)
    dma = pltpu.SemaphoreType.DMA
    vmem = pl.BlockSpec(memory_space=pltpu.VMEM)
    sketch, kernel = pl.pallas_call(
        kernel_body,
        out_shape=(
            jax.ShapeDtypeStruct((PART * ROWS, SKETCH), BF16),
            jax.ShapeDtypeStruct((NY, NZ, NC, PART * ROWS, count), F32),
        ),
        in_specs=[pl.BlockSpec(memory_space=pl.ANY), vmem, vmem, vmem],
        out_specs=(vmem, vmem),
        scratch_shapes=[
            pltpu.VMEM((PART, NX, NT) + piece, BF16),
            pltpu.VMEM((NZ, NC, NY, PART) + piece, BF16),
            pltpu.VMEM((NX, NT, PART) + piece, BF16),
            pltpu.VMEM((ROWS * BLOCK, BLOCK), F32),
            pltpu.VMEM((ROWS * SB, 2 * FAN * BLOCK), BF16),
            pltpu.VMEM((ROWS * SB, BLOCK), F32),
            pltpu.VMEM((FAN * SB, 2 * BLOCK), BF16),
            pltpu.VMEM((BLOCK, BLOCK), F32),
            pltpu.VMEM((2 * FAN * BLOCK, BLOCK), BF16),
            dma((PART,)),
            dma((PART, 7)), dma((PART, 7)),
            dma((PART, 10)), dma((PART, 10)),
            dma((PART,)), dma((PART,)),
            dma((PART,)), dma((PART,)),
            dma((PART, 2, 3)), dma((PART, 2, 3)),
            dma((PART, 2, 5)), dma((PART, 2, 5)),
        ],
        compiler_params=pltpu.CompilerParams(
            collective_id=0, has_side_effects=True, vmem_limit_bytes=56 * 2**20
        ),
        cost_estimate=pl.CostEstimate(flops=6 * 10**9, bytes_accessed=6 * 10**6, transcendentals=0),
        name="sketch_kernel",
    )(
        partials.reshape(count, -1),
        index_map.T,
        sign_bits.reshape(BLOCK, BLOCK),
        blocks,
    )
    return sketch, kernel.reshape(NY * NZ * NC, PART * ROWS, count)


def solution(mesh):
    placed = (P("group", "tensor", "shard"), P(), P(), P())
    return jax.shard_map(
        on_device,
        mesh=mesh,
        in_specs=placed,
        out_specs=(P(("group", "shard", "tensor"), None), P(None, ("shard", "tensor"), "group")),
        check_vma=False,
    )
```

time: 799 us -> 131 us (0.16); the launches traced: 787 us -> 131 us
  waiting for transfers between devices: 589 us -> 0 us
  Pallas kernels: 0 us -> 125 us
  matrix products: 107 us -> 0 us
  local copies, waits for them, and re-layouts: 67 us -> 4.99 us
  between operations: 13.9 us -> 0.64 us
    ppermute x31 -> x0, waiting for transfers between devices: 329 us -> none  [shifted(): return lax.ppermute(value, axis, pairs)]
    reduce_scatter x2 -> x0, waiting for transfers between devices: 187 us -> none  [the longest x1 133 us: on_device(): lax.psum_scatter(partial_sketch, ('shard', 'tensor'), scatter_dimension=0...]
    pallas_call x0 -> x1, Pallas kernels: none -> 125 us  [on_device(): pl.pallas_call(kernel_body, out_shape=(jax.ShapeDtypeStruct((PART * ROWS,...]
    dot_general x36 -> x0, matrix products: 107 us -> none  [the longest x32 85.7 us: tile_block(): lax.dot_general(moving, row_sketch, (((1,), (1,)), ((), ())), preferred_e...]
    all_gather x1 -> x0, waiting for transfers between devices: 72.4 us -> none  [on_device(): lax.all_gather(own_sketch, ('shard', 'tensor'), axis=0, tiled=True)]
    while x31 -> x0, local copies, waits for them, and re-layouts: 54.7 us -> none
  transfers between devices with their start and end apart: 34 -> 0, of which waited for: 34 -> 0; matrix products, arithmetic and copies ran while one was open for 0% -> 0% of each run, Pallas kernels for 0% -> 0%
where the time goes in v1:
time: 131 us
  Pallas kernels  125 us (95%)
  local copies, waits for them, and re-layouts  4.99 us (4%)
    pallas_call x1, Pallas kernels, on_device(): pl.pallas_call(kernel_body, out_shape=(jax.ShapeDtypeStruct((PART * ROWS,...  125 us
    unnamed x2, local copies, waits for them, and re-layouts  4.99 us

profile of v1, /device:TPU:1, one launch (start us, length us, event | category | flops | bytes accessed | tf_op | source)
XLA Modules:
  0.0 130.7 jit_solution(7046847417113658832)
XLA Ops:
  0.6 125.1 %sketch_kernel.1 = (bf16[48,4096]{1,0:T(8,128)(2,1)}, f32[2,8,2,48,384]{4,3,2,1,0:T(8,128)}) custom-call(bf16[384,4096]{1,0:T(8,128)(2,1)} %bitcast.5, s32[4,128]{1,0:T(4,128)} %bitcast.7, s32[128,128]{1,0:T(8,128)} %bitcast.6, bf16[4,128,128]{2,1,0:T(8,128)(2,1)} %blocks_ref.1), custom_call_target="tpu_custom_call" | custom-call | flops 6000000000 | bytes 6000000 | tf_op jit(solution)/shard_map/sketch_kernel/pallas_call | solution.py:236
  125.8 1.8 %copy.8 = bf16[48,4096]{1,0:T(8,128)(2,1)} copy(bf16[48,4096]{1,0:T(8,128)(2,1)} %get-tuple-element.8) | data formatting | bytes 786432
  127.5 3.2 %copy.9 = f32[32,48,384]{2,1,0:T(8,128)} copy(f32[32,48,384]{2,1,0:T(8,128)} %bitcast.4) | data formatting | bytes 4718592

commit v2 on v1

v2 whole, which is shorter than its diff:
```python
import math

import jax
import jax.numpy as jnp
from jax import lax
from jax.experimental import pallas as pl
from jax.experimental.pallas import tpu as pltpu
from jax.sharding import PartitionSpec as P

SKETCH = 4096
BLOCK = 128
FAN = 4
SB = SKETCH // BLOCK
NX, NT, NZ, NY, NC = 4, 2, 8, 2, 2
PART = 3
ROWS = 16
CUTS = 2
HALF = (True, False, False)
RAW = (False, True, True)
FIRST = 2
ORDER = (
    ('terms', 0, 0), ('terms', 0, 1), ('raw_sketch', 1), ('begin', 2), ('sketch', 0), ('raw_finish', 1),
    ('relay', 0), ('hop', 0, 0, 0, 1), ('hop', 0, 0, 1, 1), ('relay', 1), ('hop', 1, 0, 0, 1), ('hop', 1, 0, 1, 1),
    ('raw_sketch', 2), ('hop', 0, 0, 0, 2), ('hop', 0, 0, 1, 2), ('cross', 0, 0, 1), ('cross', 0, 1, 1),
    ('hop', 1, 1, 0, 1), ('hop', 1, 1, 1, 1), ('hop', 1, 0, 0, 2), ('hop', 1, 0, 1, 2), ('raw_finish', 2),
    ('rows_begin', 0), ('rows_begin', 1), ('rows_begin', 2), ('hop', 0, 0, 0, 3), ('hop', 0, 0, 1, 3),
    ('cross', 0, 0, 2), ('hop', 1, 1, 0, 2), ('hop', 1, 1, 1, 2), ('cross', 0, 1, 2), ('hop', 1, 0, 0, 3),
    ('hop', 1, 0, 1, 3), ('relay', 2), ('hop', 2, 0, 0, 1), ('hop', 2, 0, 1, 1), ('rows_send', 0),
    ('hop', 0, 0, 0, 4), ('hop', 0, 0, 1, 4), ('rows_send', 1), ('hop', 1, 1, 0, 3), ('hop', 1, 1, 1, 3),
    ('rows_send', 2), ('hop', 1, 0, 0, 4), ('hop', 2, 1, 1, 1), ('rows_pass', 0, 0), ('rows_pass', 0, 1),
    ('hop', 2, 1, 0, 1), ('hop', 2, 0, 1, 2), ('cross', 0, 0, 3), ('hop', 2, 0, 0, 2), ('hop', 1, 1, 1, 4),
    ('cross', 0, 1, 3), ('rows_pass', 1, 0), ('rows_pass', 1, 1), ('hop', 2, 1, 1, 2), ('cross', 0, 1, 4),
    ('hop', 2, 1, 0, 2), ('hop', 2, 0, 1, 3), ('hop', 2, 0, 0, 3), ('rows_pass', 2, 0), ('rows_pass', 2, 1),
    ('hop', 2, 1, 1, 3), ('hop', 2, 1, 0, 3), ('hop', 2, 0, 0, 4), ('rows_end',), ('siblings', 0), ('inner', 0, 0),
    ('hop', 2, 1, 1, 4), ('inner', 0, 1), ('siblings', 1), ('inner', 1, 0), ('inner', 1, 1), ('siblings', 2),
    ('inner', 2, 0), ('inner', 2, 1),
)
MESH = pl.DeviceIdType.MESH
F32 = jnp.float32
BF16 = jnp.bfloat16


def split_pair(values):
    upper = values.astype(BF16)
    return upper, (values - upper.astype(F32)).astype(BF16)


def kernel_body(
    x_ref, map_hbm, sign_hbm, blocks_hbm, sketch_ref, out_ref, map_ref, sign_ref, blocks_ref,
    mine, partner, summed_x, rx, raw, gath, rows, grad, wide, low, low_out, low_in, onehot, signs, stacked,
    local_sem, send_sem, ey_r, ex_r, el_r, sib_r, y2_r, yp_r, x_r, pass_r, z_r,
):
    group = lax.axis_index("group")
    x = lax.axis_index("shard")
    t = lax.axis_index("tensor")
    yh = group // (NZ * NC)
    z = lax.rem(group, NZ * NC) // NC
    c = lax.rem(group, NC)

    def at_group(yy, zz, cc):
        return {"group": (yy * NZ + zz) * NC + cc}

    sibling = at_group(yh, z, 1 - c)
    across = at_group(1 - yh, z, c)
    z_way = (at_group(yh, lax.rem(z + 1, NZ), c), at_group(yh, lax.rem(z + NZ - 1, NZ), c))
    other_term = {"tensor": 1 - t}

    def at_x(j):
        xx = lax.rem(x + j, NX)
        return xx, {"shard": xx}

    sent = [0, 0]

    def remote(src, dst, r, target, kind=0):
        copy = pltpu.make_async_remote_copy(
            src_ref=src, dst_ref=dst, send_sem=send_sem.at[kind], recv_sem=r, device_id=target, device_id_type=MESH
        )
        copy.start()
        sent[kind] += math.prod(src.shape) * (2 if src.dtype == F32 else 1)
        return copy

    def pieces(count):
        flat = gath.reshape(NZ * NC * NY * PART, ROWS, SKETCH)
        return flat.at[pl.ds(0, count)]

    def wait_pieces(sem, count):
        pltpu.make_async_copy(pieces(count), pieces(count), sem).wait()

    barrier = pltpu.get_barrier_semaphore()
    targets = [other_term, sibling, across, *z_way] + [at_x(j)[1] for j in (1, 2, 3)]
    for target in targets:
        pl.semaphore_signal(barrier, inc=1, device_id=target, device_id_type=MESH)
    pl.semaphore_wait(barrier, len(targets))

    def cut(p):
        return pl.ds(p * (SKETCH // CUTS), SKETCH // CUTS)

    def exchange(i, p):
        return remote(
            x_ref.at[:, 1 - t, i, :, cut(p)], partner.at[i, :, :, cut(p)], ey_r.at[i, p], other_term
        )

    def own_terms(i):
        copy = pltpu.make_async_copy(x_ref.at[:, t, i], mine.at[i], local_sem.at[i])
        copy.start()
        return copy

    def sum_terms(i, p, xx):
        return (mine[i, xx, :, cut(p)].astype(F32) + partner[i, xx, :, cut(p)].astype(F32)).astype(BF16)

    def along_shards(i, p):
        copies = []
        for j in (2, 1, 3):
            xx, target = at_x(j)
            summed_x[i, xx, :, cut(p)] = sum_terms(i, p, xx)
            copies.append(
                remote(
                    summed_x.at[i, xx, :, cut(p)], rx.at[i, x, :, cut(p)],
                    ex_r.at[i, p, j - 1], target,
                )
            )
        rx[i, x, :, cut(p)] = sum_terms(i, p, x)
        return copies

    def raw_along_shards(i, p):
        copies = []
        for j in (2, 1, 3):
            xx, target = at_x(j)
            copies.append(
                remote(
                    x_ref.at[xx, :, i, :, cut(p)], raw.at[i, x, :, :, cut(p)],
                    ex_r.at[i, p, j - 1], target,
                )
            )
        return copies

    def lay_out(source, p):
        each = SB // CUTS

        @pl.loop(0, NX)
        def _(xx):
            for b in range(p * each, (p + 1) * each):
                values = source(xx)[:, b * BLOCK:(b + 1) * BLOCK]
                grad[pl.ds(xx * SB + b, ROWS, stride=NX * SB), :] = values.astype(F32)

    def project(result):
        @pl.loop(0, ROWS // 2)
        def _(pair):
            parts = []
            for e in range(2):
                signed = grad[pl.ds(pl.multiple_of((pair * 2 + e) * BLOCK, BLOCK), BLOCK), :] * signs[...]
                parts.append(signed.astype(BF16))
            summed = jnp.dot(onehot[...], jnp.concatenate(parts, axis=1), preferred_element_type=F32)
            upper, lower = split_pair(summed)
            for e in range(2):
                place = pl.ds(pl.multiple_of((pair * 2 + e) * SB, SB), SB)
                cols = slice(e * BLOCK, (e + 1) * BLOCK)
                for f in range(FAN):
                    fr = slice(f * SB, (f + 1) * SB)
                    wide[place, f * BLOCK:(f + 1) * BLOCK] = upper[fr, cols]
                    wide[place, (FAN + f) * BLOCK:(FAN + f + 1) * BLOCK] = lower[fr, cols]

        result[...] = jnp.dot(wide[...], stacked[...], preferred_element_type=F32)

    def own_low(i):
        return low.at[pl.ds(i * ROWS * SB, ROWS * SB), :]

    def finish(i):
        for s in range(SB):
            piece = low[pl.ds(i * ROWS * SB + s, ROWS, stride=SB), :].astype(BF16)
            lanes = slice(s * BLOCK, (s + 1) * BLOCK)
            gath[z, c, yh, i, :, lanes] = piece
            rows[x, t, i, :, lanes] = piece
            sketch_ref[i * ROWS:(i + 1) * ROWS, lanes] = piece

    arrived_sibling = [0] * PART

    def to_sibling(i, block):
        arrived_sibling[i] += 1
        remote(block, block, sib_r.at[i], sibling, 1)

    from_z = {}
    from_across = {}
    from_rows = {}
    partner_rows = {}
    from_partner = {}
    from_x = {}
    low_from = {}
    own_copies = {}

    def to_across(i, w, h, block):
        from_across[i, w, h] = remote(block, block, y2_r.at[i, 0 if h == 0 else w * 3 + h], across)

    def round_z(i, k, w, h, block):
        from_z[i, k, w, h] = remote(block, block, z_r.at[i, k, w, h - 1], z_way[w])

    def place(w, h):
        return lax.rem(z + (NZ - h if w == 0 else h), NZ)

    def spread(i):
        own = gath.at[z, c, yh, i]
        for w in range(2):
            round_z(i, 0, w, 1, own)
        to_across(i, 0, 0, own)
        to_sibling(i, own)

    def relay(i):
        from_across[i, 0, 0].wait_recv()
        block = gath.at[z, c, 1 - yh, i]
        if not HALF[i]:
            for w in range(2):
                round_z(i, 1, w, 1, block)
        to_sibling(i, block)

    def hop(i, k, w, h):
        from_z[i, k, w, h].wait_recv()
        block = gath.at[place(w, h), c, yh if k == 0 else 1 - yh, i]
        if h < 3:
            round_z(i, k, w, h + 1, block)
        elif h == 3 and HALF[i]:
            round_z(i, k, w, 4, block.at[:, pl.ds(w * (SKETCH // 2), SKETCH // 2)])
        elif h == 3 and k == w:
            round_z(i, k, w, 4, block)
        if HALF[i] and h == 4 and w == 0:
            return
        if HALF[i]:
            to_across(i, w, h, block)
        to_sibling(i, block)

    def cross(i, w, h):
        from_across[i, w, h].wait_recv()
        to_sibling(i, gath.at[place(w, h), c, 1 - yh, i])

    def rows_begin(i):
        block = rows.at[x, t, i]
        partner_rows[i] = remote(block, block, yp_r.at[i], other_term)

    def rows_send(i):
        partner_rows[i].wait_recv()
        block = rows.at[x, :, i]
        for w, j in enumerate((1, 3)):
            from_rows[i, w] = remote(block, block, x_r.at[i, w], at_x(j)[1])

    def rows_pass(i, w):
        from_rows[i, w].wait_recv()
        j = (1, 3)[w]
        block = rows.at[at_x(4 - j)[0], t if w == 0 else 1 - t, i]
        remote(block, block, pass_r.at[0], at_x(j)[1])

    def rows_end():
        wait_pieces(pass_r.at[0], 2 * PART)

    def siblings(i):
        wait_pieces(sib_r.at[i], NZ * NY)

    def inner(i, q):
        left = gath[q * 4:(q + 1) * 4, :, :, i].reshape(4 * NC * NY * ROWS, SKETCH)
        right = rows[...].reshape(NX * NT * PART * ROWS, SKETCH)
        tile = lax.dot_general(left, right, (((1,), (1,)), ((), ())), preferred_element_type=F32) * (1.0 / SKETCH)
        tile = tile.reshape(4, NC, NY, ROWS, NX * NT * PART * ROWS)
        for a in range(4):
            for cc in range(NC):
                for yy in range(NY):
                    out_ref[yy, q * 4 + a, cc, i * ROWS:(i + 1) * ROWS, :] = tile[a, cc, yy]

    def begin(i):
        for p in range(CUTS):
            if RAW[i]:
                from_x[i, p] = raw_along_shards(i, p)
            else:
                from_partner[i, p] = exchange(i, p)
        if RAW[i]:
            own_copies[i] = pltpu.make_async_copy(x_ref.at[x, :, i], raw.at[i, x], local_sem.at[i])
        else:
            own_copies[i] = pltpu.make_async_copy(x_ref.at[:, t, i], mine.at[i], local_sem.at[i])
        own_copies[i].start()

    for i in range(FIRST):
        begin(i)
    small = []
    for k, (src, dst) in enumerate(((map_hbm, map_ref), (sign_hbm, sign_ref), (blocks_hbm, blocks_ref))):
        small.append(pltpu.make_async_copy(src, dst, local_sem.at[PART + k]))
        small[-1].start()
    for copy in small:
        copy.wait()

    goal = lax.broadcasted_iota(jnp.int32, (SB, BLOCK), 0)
    for f in range(FAN):
        onehot[f * SB:(f + 1) * SB, :] = jnp.where(map_ref[f:f + 1, :] == goal, 1.0, 0.0).astype(BF16)
        stacked[f * BLOCK:(f + 1) * BLOCK, :] = blocks_ref[f]
        stacked[(FAN + f) * BLOCK:(FAN + f + 1) * BLOCK, :] = blocks_ref[f]
    signs[...] = (2 * sign_ref[...] - 1).astype(F32)

    def terms(i, p):
        if p == 0:
            own_copies[i].wait()
        from_partner[i, p].wait_recv()
        from_x[i, p] = along_shards(i, p)

    def sketch(i):
        for p in range(CUTS):
            for copy in from_x[i, p]:
                copy.wait_recv()
            lay_out(lambda xx: rx.at[i, xx], p)
        project(own_low(i))
        finish(i)
        spread(i)

    def raw_sketch(i):
        own_copies[i].wait()
        for p in range(CUTS):
            for copy in from_x[i, p]:
                copy.wait_recv()
            lay_out(lambda xx: raw.at[i, xx, 1 - t], p)
        project(low_out.at[i])
        low_from[i] = remote(low_out.at[i], low_in.at[i], el_r.at[i], other_term)
        for p in range(CUTS):
            lay_out(lambda xx: raw.at[i, xx, t], p)
        project(own_low(i))

    def raw_finish(i):
        low_from[i].wait_recv()
        own_low(i)[...] = own_low(i)[...] + low_in[i]
        finish(i)
        spread(i)

    steps = {
        "begin": begin, "terms": terms, "sketch": sketch, "raw_sketch": raw_sketch, "raw_finish": raw_finish,
        "relay": relay, "hop": hop, "cross": cross, "rows_begin": rows_begin, "rows_send": rows_send,
        "rows_pass": rows_pass, "rows_end": rows_end, "siblings": siblings, "inner": inner,
    }
    for step in ORDER:
        steps[step[0]](*step[1:])

    for kind in range(2):
        wait_pieces(send_sem.at[kind], sent[kind] // (ROWS * SKETCH))


def on_device(partials, index_map, sign_bits, blocks):
    count = NX * NT * PART * ROWS
    piece = (ROWS, SKETCH)
    dma = pltpu.SemaphoreType.DMA
    vmem = pl.BlockSpec(memory_space=pltpu.VMEM)
    sketch, kernel = pl.pallas_call(
        kernel_body,
        out_shape=(
            pltpu.VMEM((PART * ROWS, SKETCH), BF16),
            pltpu.VMEM((NY, NZ, NC, PART * ROWS, count), F32),
        ),
        in_specs=[pl.BlockSpec(memory_space=pltpu.HBM)] * 4,
        out_specs=(vmem, vmem),
        scratch_shapes=[
            pltpu.VMEM(index_map.shape[::-1], jnp.int32),
            pltpu.VMEM((BLOCK, BLOCK), jnp.int32),
            pltpu.VMEM(blocks.shape, BF16),
            pltpu.VMEM((PART, NX) + piece, BF16),
            pltpu.VMEM((PART, NX) + piece, BF16),
            pltpu.VMEM((PART, NX) + piece, BF16),
            pltpu.VMEM((PART, NX) + piece, BF16),
            pltpu.VMEM((PART, NX, NT) + piece, BF16),
            pltpu.VMEM((NZ, NC, NY, PART) + piece, BF16),
            pltpu.VMEM((NX, NT, PART) + piece, BF16),
            pltpu.VMEM((ROWS * BLOCK, BLOCK), F32),
            pltpu.VMEM((ROWS * SB, 2 * FAN * BLOCK), BF16),
            pltpu.VMEM((PART * ROWS * SB, BLOCK), F32),
            pltpu.VMEM((PART, ROWS * SB, BLOCK), F32),
            pltpu.VMEM((PART, ROWS * SB, BLOCK), F32),
            pltpu.VMEM((FAN * SB, BLOCK), BF16),
            pltpu.VMEM((BLOCK, BLOCK), F32),
            pltpu.VMEM((2 * FAN * BLOCK, BLOCK), BF16),
            dma((PART + 3,)), dma((2,)),
            dma((PART, CUTS)), dma((PART, CUTS, 3)), dma((PART,)), dma((PART,)),
            dma((PART, 8)), dma((PART,)), dma((PART, 2)), dma((1,)), dma((PART, 2, 2, 4)),
        ],
        compiler_params=pltpu.CompilerParams(
            collective_id=0, has_side_effects=True, vmem_limit_bytes=56 * 2**20
        ),
        cost_estimate=pl.CostEstimate(flops=6 * 10**9, bytes_accessed=6 * 10**6, transcendentals=0),
        name="sketch_kernel",
    )(
        partials.reshape(NX, NT, PART, ROWS, -1),
        index_map.T,
        sign_bits.reshape(BLOCK, BLOCK),
        blocks,
    )
    return sketch, kernel.reshape(NY * NZ * NC, PART * ROWS, count)


def solution(mesh):
    placed = (P("group", "tensor", "shard"), P(), P(), P())
    return jax.shard_map(
        on_device,
        mesh=mesh,
        in_specs=placed,
        out_specs=(P(("group", "shard", "tensor"), None), P(None, ("shard", "tensor"), "group")),
        check_vma=False,
    )
```

time: 131 us -> 95.6 us (0.73)
  Pallas kernels: 125 us -> 92.1 us
  local copies, waits for them, and re-layouts: 4.99 us -> 2.15 us
    pallas_call x1, Pallas kernels: 125 us -> 92.1 us  [on_device(): pl.pallas_call(kernel_body, out_shape=(pltpu.VMEM((PART * ROWS, SKETCH),...]
    unnamed x2, local copies, waits for them, and re-layouts: 4.99 us -> 2.15 us
where the time goes in v2:
time: 95.6 us; the launch traced here: 94.9 us
  Pallas kernels  92.1 us (96%)
  local copies, waits for them, and re-layouts  2.15 us (2%)
    pallas_call x1, Pallas kernels, on_device(): pl.pallas_call(kernel_body, out_shape=(pltpu.VMEM((PART * ROWS, SKETCH),...  92.1 us
    unnamed x2, local copies, waits for them, and re-layouts  2.15 us

profile of v2, /device:TPU:1, one launch (start us, length us, event | category | flops | bytes accessed | tf_op | source)
XLA Modules:
  0.0 94.9 jit_solution(10675577442158838918)
XLA Ops:
  0.6 92.1 %sketch_kernel.1 = (bf16[48,4096]{1,0:T(8,128)(2,1)S(1)}, f32[2,8,2,48,384]{4,3,2,1,0:T(8,128)S(1)}) custom-call(bf16[4,2,3,16,4096]{4,3,2,1,0:T(8,128)(2,1)} %bitcast.5, s32[4,128]{1,0:T(4,128)} %bitcast.7, s32[128,128]{1,0:T(8,128)} %bitcast.6, bf16[4,128,128]{2,1,0:T(8,128)(2,1)} %blocks_hbm.1), custom_call_target="tpu_custom_call" | custom-call | flops 6000000000 | bytes 6000000 | tf_op jit(solution)/shard_map/sketch_kernel/pallas_call | solution.py:344
  92.8 0.7 copy.8
  93.5 1.4 %copy.9 = f32[32,48,384]{2,1,0:T(8,128)} copy(f32[32,48,384]{2,1,0:T(8,128)S(1)} %bitcast.4) | data formatting | bytes 4718592

commit v3 on v2

--- a/solution.py
+++ b/solution.py
@@ -14,26 +14,26 @@
 NX, NT, NZ, NY, NC = 4, 2, 8, 2, 2
 PART = 3
 ROWS = 16
-CUTS = 2
+CUTS = 4
 HALF = (True, False, False)
-RAW = (False, True, True)
+RAW = (False, True, False)
 FIRST = 2
 ORDER = (
-    ('terms', 0, 0), ('terms', 0, 1), ('raw_sketch', 1), ('begin', 2), ('sketch', 0), ('raw_finish', 1),
-    ('relay', 0), ('hop', 0, 0, 0, 1), ('hop', 0, 0, 1, 1), ('relay', 1), ('hop', 1, 0, 0, 1), ('hop', 1, 0, 1, 1),
-    ('raw_sketch', 2), ('hop', 0, 0, 0, 2), ('hop', 0, 0, 1, 2), ('cross', 0, 0, 1), ('cross', 0, 1, 1),
-    ('hop', 1, 1, 0, 1), ('hop', 1, 1, 1, 1), ('hop', 1, 0, 0, 2), ('hop', 1, 0, 1, 2), ('raw_finish', 2),
-    ('rows_begin', 0), ('rows_begin', 1), ('rows_begin', 2), ('hop', 0, 0, 0, 3), ('hop', 0, 0, 1, 3),
-    ('cross', 0, 0, 2), ('hop', 1, 1, 0, 2), ('hop', 1, 1, 1, 2), ('cross', 0, 1, 2), ('hop', 1, 0, 0, 3),
-    ('hop', 1, 0, 1, 3), ('relay', 2), ('hop', 2, 0, 0, 1), ('hop', 2, 0, 1, 1), ('rows_send', 0),
-    ('hop', 0, 0, 0, 4), ('hop', 0, 0, 1, 4), ('rows_send', 1), ('hop', 1, 1, 0, 3), ('hop', 1, 1, 1, 3),
-    ('rows_send', 2), ('hop', 1, 0, 0, 4), ('hop', 2, 1, 1, 1), ('rows_pass', 0, 0), ('rows_pass', 0, 1),
-    ('hop', 2, 1, 0, 1), ('hop', 2, 0, 1, 2), ('cross', 0, 0, 3), ('hop', 2, 0, 0, 2), ('hop', 1, 1, 1, 4),
-    ('cross', 0, 1, 3), ('rows_pass', 1, 0), ('rows_pass', 1, 1), ('hop', 2, 1, 1, 2), ('cross', 0, 1, 4),
-    ('hop', 2, 1, 0, 2), ('hop', 2, 0, 1, 3), ('hop', 2, 0, 0, 3), ('rows_pass', 2, 0), ('rows_pass', 2, 1),
-    ('hop', 2, 1, 1, 3), ('hop', 2, 1, 0, 3), ('hop', 2, 0, 0, 4), ('rows_end',), ('siblings', 0), ('inner', 0, 0),
-    ('hop', 2, 1, 1, 4), ('inner', 0, 1), ('siblings', 1), ('inner', 1, 0), ('inner', 1, 1), ('siblings', 2),
-    ('inner', 2, 0), ('inner', 2, 1),
+    ('terms', 0, 0), ('terms', 0, 1), ('terms', 0, 2), ('terms', 0, 3), ('begin', 2), ('raw_sketch', 1),
+    ('sketch', 0), ('terms', 2, 0), ('terms', 2, 1), ('terms', 2, 2), ('terms', 2, 3), ('rows_begin', 0),
+    ('hop', 0, 0, 0, 1), ('hop', 0, 0, 1, 1), ('sketch', 2), ('raw_finish', 1), ('rows_begin', 1),
+    ('rows_begin', 2), ('hop', 0, 0, 0, 2), ('hop', 0, 0, 1, 2), ('relay', 0), ('rows_send', 0),
+    ('hop', 2, 0, 0, 1), ('hop', 2, 0, 1, 1), ('cross', 0, 0, 1), ('hop', 1, 0, 1, 1), ('hop', 1, 0, 0, 1),
+    ('cross', 0, 1, 1), ('rows_pass', 0, 0), ('rows_pass', 0, 1), ('hop', 0, 0, 0, 3), ('hop', 0, 0, 1, 3),
+    ('relay', 2), ('hop', 2, 0, 0, 2), ('hop', 2, 0, 1, 2), ('relay', 1), ('hop', 1, 0, 1, 2), ('hop', 1, 0, 0, 2),
+    ('hop', 0, 0, 0, 4), ('hop', 0, 0, 1, 4), ('rows_send', 1), ('hop', 2, 1, 1, 1), ('hop', 2, 1, 0, 1),
+    ('rows_send', 2), ('hop', 2, 0, 0, 3), ('hop', 2, 0, 1, 3), ('cross', 0, 0, 2), ('rows_pass', 1, 1),
+    ('rows_pass', 1, 0), ('hop', 1, 1, 1, 1), ('hop', 1, 1, 0, 1), ('cross', 0, 1, 2), ('hop', 1, 0, 1, 3),
+    ('hop', 1, 0, 0, 3), ('cross', 0, 0, 3), ('rows_pass', 2, 1), ('rows_pass', 2, 0), ('hop', 2, 1, 1, 2),
+    ('hop', 2, 1, 0, 2), ('cross', 0, 1, 3), ('hop', 1, 1, 1, 2), ('hop', 2, 0, 0, 4), ('cross', 0, 1, 4),
+    ('rows_end',), ('inner', 0, 0), ('hop', 1, 1, 0, 2), ('hop', 2, 1, 1, 3), ('inner', 0, 1), ('inner', 1, 0),
+    ('hop', 1, 1, 1, 3), ('hop', 1, 0, 0, 4), ('inner', 2, 0), ('hop', 2, 1, 0, 3), ('hop', 2, 1, 1, 4),
+    ('inner', 2, 1), ('hop', 1, 1, 0, 3), ('hop', 1, 1, 1, 4), ('inner', 1, 1),
 )
 MESH = pl.DeviceIdType.MESH
 F32 = jnp.float32
@@ -173,11 +173,8 @@
             rows[x, t, i, :, lanes] = piece
             sketch_ref[i * ROWS:(i + 1) * ROWS, lanes] = piece
 
-    arrived_sibling = [0] * PART
-
-    def to_sibling(i, block):
-        arrived_sibling[i] += 1
-        remote(block, block, sib_r.at[i], sibling, 1)
+    def to_sibling(i, block, h):
+        remote(block, block, sib_r.at[i, 0 if h < 3 else 1], sibling, 1)
 
     from_z = {}
     from_across = {}
@@ -202,7 +199,7 @@
         for w in range(2):
             round_z(i, 0, w, 1, own)
         to_across(i, 0, 0, own)
-        to_sibling(i, own)
+        to_sibling(i, own, 0)
 
     def relay(i):
         from_across[i, 0, 0].wait_recv()
@@ -210,7 +207,7 @@
         if not HALF[i]:
             for w in range(2):
                 round_z(i, 1, w, 1, block)
-        to_sibling(i, block)
+        to_sibling(i, block, 0)
 
     def hop(i, k, w, h):
         from_z[i, k, w, h].wait_recv()
@@ -225,11 +222,11 @@
             return
         if HALF[i]:
             to_across(i, w, h, block)
-        to_sibling(i, block)
+        to_sibling(i, block, h)
 
     def cross(i, w, h):
         from_across[i, w, h].wait_recv()
-        to_sibling(i, gath.at[place(w, h), c, 1 - yh, i])
+        to_sibling(i, gath.at[place(w, h), c, 1 - yh, i], h)
 
     def rows_begin(i):
         block = rows.at[x, t, i]
@@ -250,18 +247,18 @@
     def rows_end():
         wait_pieces(pass_r.at[0], 2 * PART)
 
-    def siblings(i):
-        wait_pieces(sib_r.at[i], NZ * NY)
-
-    def inner(i, q):
-        left = gath[q * 4:(q + 1) * 4, :, :, i].reshape(4 * NC * NY * ROWS, SKETCH)
+    def inner(i, late):
+        wait_pieces(sib_r.at[i, late], (10, 6)[late])
+        turns = ((0, 1, 7, 2, 6), (3, 5, 4))[late]
+        spots = [lax.rem(z + turn, NZ) for turn in turns]
+        left = jnp.concatenate([gath[zz, :, :, i].reshape(NC * NY * ROWS, SKETCH) for zz in spots], axis=0)
         right = rows[...].reshape(NX * NT * PART * ROWS, SKETCH)
         tile = lax.dot_general(left, right, (((1,), (1,)), ((), ())), preferred_element_type=F32) * (1.0 / SKETCH)
-        tile = tile.reshape(4, NC, NY, ROWS, NX * NT * PART * ROWS)
-        for a in range(4):
+        tile = tile.reshape(len(turns), NC, NY, ROWS, NX * NT * PART * ROWS)
+        for a, zz in enumerate(spots):
             for cc in range(NC):
                 for yy in range(NY):
-                    out_ref[yy, q * 4 + a, cc, i * ROWS:(i + 1) * ROWS, :] = tile[a, cc, yy]
+                    out_ref[yy, zz, cc, i * ROWS:(i + 1) * ROWS, :] = tile[a, cc, yy]
 
     def begin(i):
         for p in range(CUTS):
@@ -327,7 +324,7 @@
     steps = {
         "begin": begin, "terms": terms, "sketch": sketch, "raw_sketch": raw_sketch, "raw_finish": raw_finish,
         "relay": relay, "hop": hop, "cross": cross, "rows_begin": rows_begin, "rows_send": rows_send,
-        "rows_pass": rows_pass, "rows_end": rows_end, "siblings": siblings, "inner": inner,
+        "rows_pass": rows_pass, "rows_end": rows_end, "inner": inner,
     }
     for step in ORDER:
         steps[step[0]](*step[1:])
@@ -369,8 +366,8 @@
             pltpu.VMEM((BLOCK, BLOCK), F32),
             pltpu.VMEM((2 * FAN * BLOCK, BLOCK), BF16),
             dma((PART + 3,)), dma((2,)),
-            dma((PART, CUTS)), dma((PART, CUTS, 3)), dma((PART,)), dma((PART,)),
-            dma((PART, 8)), dma((PART,)), dma((PART, 2)), dma((1,)), dma((PART, 2, 2, 4)),
+            dma((PART, CUTS)), dma((PART, CUTS, 3)), dma((PART,)),
+            dma((PART, 2)), dma((PART, 8)), dma((PART,)), dma((PART, 2)), dma((1,)), dma((PART, 2, 2, 4)),
         ],
         compiler_params=pltpu.CompilerParams(
             collective_id=0, has_side_effects=True, vmem_limit_bytes=56 * 2**20

time: 95.6 us -> 94 us (0.983)
    pallas_call x1, Pallas kernels: 92.1 us -> 91.2 us  [on_device(): pl.pallas_call(kernel_body, out_shape=(pltpu.VMEM((PART * ROWS, SKETCH),...]
where the time goes in v3:
time: 94 us; the launch traced here: 93.9 us
  Pallas kernels  91.2 us (97%)
  local copies, waits for them, and re-layouts  2.15 us (2%)
    pallas_call x1, Pallas kernels, on_device(): pl.pallas_call(kernel_body, out_shape=(pltpu.VMEM((PART * ROWS, SKETCH),...  91.2 us
    unnamed x2, local copies, waits for them, and re-layouts  2.15 us

profile of v3, /device:TPU:1, one launch (start us, length us, event | category | flops | bytes accessed | tf_op | source)
XLA Modules:
  0.0 93.9 jit_solution(3806513086260511997)
XLA Ops:
  0.6 91.2 %sketch_kernel.1 = (bf16[48,4096]{1,0:T(8,128)(2,1)S(1)}, f32[2,8,2,48,384]{4,3,2,1,0:T(8,128)S(1)}) custom-call(bf16[4,2,3,16,4096]{4,3,2,1,0:T(8,128)(2,1)} %bitcast.5, s32[4,128]{1,0:T(4,128)} %bitcast.7, s32[128,128]{1,0:T(8,128)} %bitcast.6, bf16[4,128,128]{2,1,0:T(8,128)(2,1)} %blocks_hbm.1), custom_call_target="tpu_custom_call" | custom-call | flops 6000000000 | bytes 6000000 | tf_op jit(solution)/shard_map/sketch_kernel/pallas_call | solution.py:341
  91.8 0.7 copy.8
  92.5 1.4 %copy.9 = f32[32,48,384]{2,1,0:T(8,128)} copy(f32[32,48,384]{2,1,0:T(8,128)S(1)} %bitcast.4) | data formatting | bytes 4718592

commit v4 on v3

--- a/solution.py
+++ b/solution.py
@@ -16,24 +16,24 @@
 ROWS = 16
 CUTS = 4
 HALF = (True, False, False)
-RAW = (False, True, False)
-FIRST = 2
+RAW = (False, False, True)
+FIRST = 1
 ORDER = (
-    ('terms', 0, 0), ('terms', 0, 1), ('terms', 0, 2), ('terms', 0, 3), ('begin', 2), ('raw_sketch', 1),
-    ('sketch', 0), ('terms', 2, 0), ('terms', 2, 1), ('terms', 2, 2), ('terms', 2, 3), ('rows_begin', 0),
-    ('hop', 0, 0, 0, 1), ('hop', 0, 0, 1, 1), ('sketch', 2), ('raw_finish', 1), ('rows_begin', 1),
-    ('rows_begin', 2), ('hop', 0, 0, 0, 2), ('hop', 0, 0, 1, 2), ('relay', 0), ('rows_send', 0),
-    ('hop', 2, 0, 0, 1), ('hop', 2, 0, 1, 1), ('cross', 0, 0, 1), ('hop', 1, 0, 1, 1), ('hop', 1, 0, 0, 1),
-    ('cross', 0, 1, 1), ('rows_pass', 0, 0), ('rows_pass', 0, 1), ('hop', 0, 0, 0, 3), ('hop', 0, 0, 1, 3),
-    ('relay', 2), ('hop', 2, 0, 0, 2), ('hop', 2, 0, 1, 2), ('relay', 1), ('hop', 1, 0, 1, 2), ('hop', 1, 0, 0, 2),
-    ('hop', 0, 0, 0, 4), ('hop', 0, 0, 1, 4), ('rows_send', 1), ('hop', 2, 1, 1, 1), ('hop', 2, 1, 0, 1),
-    ('rows_send', 2), ('hop', 2, 0, 0, 3), ('hop', 2, 0, 1, 3), ('cross', 0, 0, 2), ('rows_pass', 1, 1),
-    ('rows_pass', 1, 0), ('hop', 1, 1, 1, 1), ('hop', 1, 1, 0, 1), ('cross', 0, 1, 2), ('hop', 1, 0, 1, 3),
-    ('hop', 1, 0, 0, 3), ('cross', 0, 0, 3), ('rows_pass', 2, 1), ('rows_pass', 2, 0), ('hop', 2, 1, 1, 2),
-    ('hop', 2, 1, 0, 2), ('cross', 0, 1, 3), ('hop', 1, 1, 1, 2), ('hop', 2, 0, 0, 4), ('cross', 0, 1, 4),
-    ('rows_end',), ('inner', 0, 0), ('hop', 1, 1, 0, 2), ('hop', 2, 1, 1, 3), ('inner', 0, 1), ('inner', 1, 0),
-    ('hop', 1, 1, 1, 3), ('hop', 1, 0, 0, 4), ('inner', 2, 0), ('hop', 2, 1, 0, 3), ('hop', 2, 1, 1, 4),
-    ('inner', 2, 1), ('hop', 1, 1, 0, 3), ('hop', 1, 1, 1, 4), ('inner', 1, 1),
+    ('begin', 2), ('terms', 0, 0), ('terms', 0, 1), ('terms', 0, 2), ('terms', 0, 3), ('begin', 1),
+    ('raw_sketch', 2), ('raw_own', 2), ('terms', 1, 0), ('terms', 1, 1), ('sketch', 0), ('terms', 1, 2),
+    ('terms', 1, 3), ('rows_begin', 0), ('hop', 0, 0, 0, 1), ('hop', 0, 0, 1, 1), ('sketch', 1), ('raw_finish', 2),
+    ('rows_begin', 1), ('rows_begin', 2), ('hop', 0, 0, 1, 2), ('hop', 0, 0, 0, 2), ('relay', 0), ('rows_send', 0),
+    ('hop', 1, 0, 1, 1), ('hop', 1, 0, 0, 1), ('cross', 0, 0, 1), ('hop', 2, 0, 0, 1), ('hop', 2, 0, 1, 1),
+    ('cross', 0, 1, 1), ('rows_pass', 0, 0), ('rows_pass', 0, 1), ('hop', 0, 0, 1, 3), ('hop', 0, 0, 0, 3),
+    ('relay', 1), ('hop', 1, 0, 1, 2), ('hop', 1, 0, 0, 2), ('relay', 2), ('hop', 2, 0, 1, 2), ('hop', 2, 0, 0, 2),
+    ('hop', 0, 0, 0, 4), ('hop', 0, 0, 1, 4), ('rows_send', 1), ('hop', 1, 1, 0, 1), ('hop', 1, 1, 1, 1),
+    ('rows_send', 2), ('hop', 1, 0, 1, 3), ('hop', 1, 0, 0, 3), ('cross', 0, 1, 2), ('rows_pass', 1, 1),
+    ('rows_pass', 1, 0), ('hop', 2, 1, 0, 1), ('hop', 2, 1, 1, 1), ('cross', 0, 0, 2), ('hop', 2, 0, 0, 3),
+    ('hop', 2, 0, 1, 3), ('cross', 0, 1, 3), ('rows_pass', 2, 0), ('rows_pass', 2, 1), ('hop', 1, 1, 0, 2),
+    ('hop', 1, 1, 1, 2), ('cross', 0, 0, 3), ('hop', 1, 0, 0, 4), ('hop', 2, 1, 1, 2), ('cross', 0, 1, 4),
+    ('rows_end',), ('inner', 0, 0), ('hop', 1, 1, 1, 3), ('hop', 2, 1, 0, 2), ('inner', 0, 1), ('inner', 1, 0),
+    ('hop', 2, 1, 1, 3), ('hop', 2, 0, 0, 4), ('inner', 2, 0), ('hop', 1, 1, 0, 3), ('hop', 1, 1, 1, 4),
+    ('inner', 1, 1), ('hop', 2, 1, 0, 3), ('hop', 2, 1, 1, 4), ('inner', 2, 1),
 )
 MESH = pl.DeviceIdType.MESH
 F32 = jnp.float32
@@ -311,6 +311,8 @@
             lay_out(lambda xx: raw.at[i, xx, 1 - t], p)
         project(low_out.at[i])
         low_from[i] = remote(low_out.at[i], low_in.at[i], el_r.at[i], other_term)
+
+    def raw_own(i):
         for p in range(CUTS):
             lay_out(lambda xx: raw.at[i, xx, t], p)
         project(own_low(i))
@@ -322,7 +324,7 @@
         spread(i)
 
     steps = {
-        "begin": begin, "terms": terms, "sketch": sketch, "raw_sketch": raw_sketch, "raw_finish": raw_finish,
+        "begin": begin, "terms": terms, "sketch": sketch, "raw_sketch": raw_sketch, "raw_own": raw_own, "raw_finish": raw_finish,
         "relay": relay, "hop": hop, "cross": cross, "rows_begin": rows_begin, "rows_send": rows_send,
         "rows_pass": rows_pass, "rows_end": rows_end, "inner": inner,
     }

time: 94 us -> 93.1 us (level)
  Pallas kernels: 91.2 us -> 90.2 us
where the time goes in v4:
time: 93.1 us; the launch traced here: 93 us
  Pallas kernels  90.2 us (97%)
  local copies, waits for them, and re-layouts  2.15 us (2%)
    pallas_call x1, Pallas kernels, on_device(): pl.pallas_call(kernel_body, out_shape=(pltpu.VMEM((PART * ROWS, SKETCH),...  90.2 us
    unnamed x2, local copies, waits for them, and re-layouts  2.15 us

profile of v4, /device:TPU:1, one launch (start us, length us, event | category | flops | bytes accessed | tf_op | source)
XLA Modules:
  0.0 93.0 jit_solution(14457899053675091774)
XLA Ops:
  0.6 90.2 %sketch_kernel.1 = (bf16[48,4096]{1,0:T(8,128)(2,1)S(1)}, f32[2,8,2,48,384]{4,3,2,1,0:T(8,128)S(1)}) custom-call(bf16[4,2,3,16,4096]{4,3,2,1,0:T(8,128)(2,1)} %bitcast.5, s32[4,128]{1,0:T(4,128)} %bitcast.7, s32[128,128]{1,0:T(8,128)} %bitcast.6, bf16[4,128,128]{2,1,0:T(8,128)(2,1)} %blocks_hbm.1), custom_call_target="tpu_custom_call" | custom-call | flops 6000000000 | bytes 6000000 | tf_op jit(solution)/shard_map/sketch_kernel/pallas_call | solution.py:343
  90.9 0.7 copy.8
  91.6 1.4 %copy.9 = f32[32,48,384]{2,1,0:T(8,128)} copy(f32[32,48,384]{2,1,0:T(8,128)S(1)} %bitcast.4) | data formatting | bytes 4718592
